TPU v7x, 256 devices: a whole 4x4x8 slice. The times are simulated.
256 devices in a mesh: dp: 16 (over y, z_lo), tensor: 16 (over z_hi, x, core).
Axes of the slice: x: 4, y: 4, z: 8 (z_hi: 2, z_lo: 4; z = z_hi * 4 + z_lo), core: 2. Of those that a mesh axis runs over, the one named last changes fastest.
Arguments:
- tokens: bfloat16 [4096, 4096], P('dp'), may hold values from -6 to 6
- cotangent: bfloat16 [4096, 4096], P('dp'), may hold values from -0.1875 to 0.1875
- up_weight_kept: bfloat16 [4096, 14336], P('dp', 'tensor'), may hold values from -0.09375 to 0.09375
- down_weight_kept: bfloat16 [4096, 14336], P('dp', 'tensor'), may hold values from -0.09375 to 0.09375
- first_moment_blocks: float32 [2, 4096, 14336], P(None, 'dp', 'tensor'), may hold values from -6 to 6
- second_moment_blocks: float32 [2, 4096, 14336], P(None, 'dp', 'tensor'), may hold values from 0.5 to 5
- block_destination: int32 [16, 16], replicated, may hold values from 0 to 15, as said below
- surviving_device_rank: int32 [16], replicated, may hold values from 0 to 15, each once
Outputs:
- new_up: bfloat16 [4096, 14336], P('dp', 'tensor')
- new_down: bfloat16 [4096, 14336], P('dp', 'tensor')
- new_first: float32 [2, 4096, 14336], P(None, 'dp', 'tensor')
- new_second: float32 [2, 4096, 14336], P(None, 'dp', 'tensor')
Inputs may be any that keep to these rules, and one draw needn't show every extreme that they name: Each row of block_destination names every new tensor index exactly once.
All inputs are finite; a program needn't handle non-finite values.
Results may differ from a plain program's by a relative error of at most 0.0035.
Values may be sent and summed in bfloat16 or wider, within the bound.
A program may use at most 128 MiB of HBM per device.

v0:
```python
import jax
import jax.numpy as jnp
from jax import lax
from jax.sharding import PartitionSpec as P

beta_first = 0.9
beta_second = 0.95
adam_eps = 1e-08
rate = 0.005
step_count = 20


def rounded(value):
    return lax.optimization_barrier(value.astype(jnp.bfloat16)).astype(jnp.float32)


def adam(weight, first, second, grad):
    first_new = beta_first * first + (1.0 - beta_first) * grad
    second_new = beta_second * second + (1.0 - beta_second) * grad * grad
    first_hat = first_new / (1.0 - beta_first**step_count)
    second_hat = second_new / (1.0 - beta_second**step_count)
    updated = weight.astype(jnp.float32) - rate * first_hat / (jnp.sqrt(second_hat) + adam_eps)
    return (updated.astype(jnp.bfloat16), first_new, second_new)


def per_device(
    tokens,
    cotangent,
    up_weight_kept,
    down_weight_kept,
    first_moment_blocks,
    second_moment_blocks,
    block_destination,
    surviving_device_rank,
):
    tensor_groups = lax.axis_size("tensor")
    group_member = lax.axis_index("tensor")
    rows_dev, width = up_weight_kept.shape
    piece = rows_dev // tensor_groups
    tok_rows = tokens.shape[0]
    block_positions = jnp.arange(tensor_groups, dtype=jnp.int32)
    own_row = lax.dynamic_index_in_dim(block_destination, group_member, 0, keepdims=False)
    send_order = jnp.sum(
        block_positions[None, :] * (own_row[None, :] == block_positions[:, None]).astype(jnp.int32),
        axis=1,
    )
    placed_blocks = (surviving_device_rank + group_member) % tensor_groups
    recv_pick = jnp.sum(
        block_positions[:, None]
        * (placed_blocks[:, None] == block_positions[None, :]).astype(jnp.int32),
        axis=0,
    )
    outgoing = jnp.take(
        jnp.stack([up_weight_kept, down_weight_kept]).reshape(2, tensor_groups, piece, width),
        send_order,
        axis=1,
    )
    incoming = lax.all_to_all(outgoing, "tensor", split_axis=1, concat_axis=1, tiled=True)
    weights = jnp.take(incoming, recv_pick, axis=1).reshape(2, rows_dev, width)
    first_out = jnp.take(
        first_moment_blocks.reshape(2, tensor_groups, piece, width), send_order, axis=1
    )
    second_out = jnp.take(
        second_moment_blocks.reshape(2, tensor_groups, piece, width), send_order, axis=1
    )
    first_in, second_in = (
        lax.all_to_all(first_out, "tensor", split_axis=1, concat_axis=1, tiled=True),
        lax.all_to_all(second_out, "tensor", split_axis=1, concat_axis=1, tiled=True),
    )
    first_now = jnp.take(first_in, recv_pick, axis=1).reshape(2, rows_dev, width)
    second_now = jnp.take(second_in, recv_pick, axis=1).reshape(2, rows_dev, width)
    up_weight = weights[0]
    down_weight = weights[1]
    up_piece = lax.all_gather(up_weight, "dp", axis=0, tiled=True)
    down_piece = lax.all_gather(down_weight, "dp", axis=0, tiled=True)
    count = up_piece.shape[0] // rows_dev
    cols_x = tokens.reshape(tok_rows, count, rows_dev)
    cols_dy = cotangent.reshape(tok_rows, count, rows_dev)
    up_part = jnp.einsum(
        "rkd,kdf->krf",
        cols_x,
        up_piece.reshape(count, rows_dev, width),
        preferred_element_type=jnp.float32,
    )
    down_part = jnp.einsum(
        "rkd,kdf->krf",
        cols_dy,
        down_piece.reshape(count, rows_dev, width),
        preferred_element_type=jnp.float32,
    )
    pre = jnp.sum(rounded(up_part), axis=0)
    back = jnp.sum(rounded(down_part), axis=0)
    sigma = jax.nn.sigmoid(pre)
    hidden = (pre * sigma).astype(jnp.bfloat16)
    slope = (back * sigma * (1.0 + pre * (1.0 - sigma))).astype(jnp.bfloat16)
    cols_x = tokens
    cols_dy = cotangent
    grads = lax.psum_scatter(
        jnp.concatenate(
            [
                jnp.einsum("rd,rf->df", cols_x, slope, preferred_element_type=jnp.float32),
                jnp.einsum("rd,rf->df", cols_dy, hidden, preferred_element_type=jnp.float32),
            ],
            axis=1,
        ).astype(jnp.bfloat16),
        "dp",
        scatter_dimension=0,
        tiled=True,
    ).astype(jnp.float32)
    grad_up = grads[:, :width]
    grad_down = grads[:, width:]
    new_up, f_up, s_up = adam(up_weight, first_now[0], second_now[0], grad_up)
    new_down, f_down, s_down = adam(down_weight, first_now[1], second_now[1], grad_down)
    return (new_up, new_down, jnp.stack([f_up, f_down]), jnp.stack([s_up, s_down]))


def solution(mesh):
    in_specs = (
        P("dp", None),
        P("dp", None),
        P("dp", "tensor"),
        P("dp", "tensor"),
        P(None, "dp", "tensor"),
        P(None, "dp", "tensor"),
        P(),
        P(),
    )
    out_specs = (
        P("dp", "tensor"),
        P("dp", "tensor"),
        P(None, "dp", "tensor"),
        P(None, "dp", "tensor"),
    )
    return jax.shard_map(
        per_device, mesh=mesh, in_specs=in_specs, out_specs=out_specs, check_vma=False
    )
```

profile of v0, /device:TPU:34, one launch (start us, length us, event | category | flops | bytes accessed | tf_op | source)
XLA Modules:
  0.0 823.7 jit_solution(15063862041483045758)
XLA Ops:
  13.3 10.6 %all-to-all-start = ((bf16[2,16,16,896]{3,2,0,1:T(8,128)(2,1)}), bf16[2,16,16,896]{3,2,0,1:T(8,128)(2,1)S(1)}, u32[]{:S(2)}, u32[]{:S(2)}) async-start(bf16[2,16,16,896]{3,2,0,1:T(8,128)(2,1)} %select_bitcast_fusion.5), calls=%async_computation | async-start | bytes 1835008 | tf_op jit(solution)/shard_map/all_to_all | solution.py:58
  24.0 24.3 %all-to-all-done = bf16[2,16,16,896]{3,2,0,1:T(8,128)(2,1)S(1)} async-done(((bf16[2,16,16,896]{3,2,0,1:T(8,128)(2,1)}), bf16[2,16,16,896]{3,2,0,1:T(8,128)(2,1)S(1)}, u32[]{:S(2)}, u32[]{:S(2)}) %all-to-all-start) | async-done | bytes 917536 | tf_op jit(solution)/shard_map/all_to_all | solution.py:58
  53.2 160.8 %all-gather.3.cloned.1.call-done = bf16[4096,896]{1,0:T(8,128)(2,1)} async-done(((bf16[256,896]{1,0:T(8,128)(2,1)}), bf16[4096,896]{1,0:T(8,128)(2,1)}) %all-gather.3.cloned.1.call-update) | async-done | bytes 7340048 | tf_op jit(solution)/shard_map/all_gather | solution.py:75
  213.9 9.0 %convert_bitcast_fusion.3 = bf16[16,256,896]{1,2,0:T(8,128)(2,1)} fusion(bf16[16,256,896]{2,1,0:T(8,128)(2,1)} %bitcast.56, bf16[32,16,8,256]{3,2,1,0:T(8,128)(2,1)} %bitcast.66), kind=kOutput, calls=%fused_computation.12 | convolution fusion | flops 1882718208 | bytes 16777216 | tf_op jit(solution)/shard_map/rkd,kdf->krf/dot_general | solution.py:85
  222.9 155.8 %all-gather.5.cloned.1.call-done = bf16[4096,896]{1,0:T(8,128)(2,1)} async-done(((bf16[256,896]{1,0:T(8,128)(2,1)}), bf16[4096,896]{1,0:T(8,128)(2,1)}) %all-gather.5.cloned.1.call-update) | async-done | bytes 7340048 | tf_op jit(solution)/shard_map/all_gather | solution.py:74
  378.8 8.9 %convert_bitcast_fusion.2 = bf16[16,256,896]{1,2,0:T(8,128)(2,1)} fusion(bf16[16,256,896]{2,1,0:T(8,128)(2,1)} %bitcast.57, bf16[32,16,8,256]{3,2,1,0:T(8,128)(2,1)} %bitcast.55), kind=kOutput, calls=%fused_computation.11 | convolution fusion | flops 1882718208 | bytes 16777216 | tf_op jit(solution)/shard_map/rkd,kdf->krf/dot_general | solution.py:79
  387.7 7.5 convert_reduce_fusion
  399.6 13.1 %pad_maximum_fusion = bf16[4096,1792]{0,1:T(8,128)(2,1)} fusion(bf16[4096,896]{0,1:T(8,128)(2,1)S(1)} %convert_bitcast_fusion, bf16[4096,896]{0,1:T(8,128)(2,1)S(1)} %convert_bitcast_fusion.1), kind=kLoop, calls=%fused_computation.6 | loop fusion | flops 29360128 | bytes 29360128 | tf_op jit(solution)/shard_map/concatenate | solution.py:99
  414.5 3.4 gather_fusion.2
  417.9 3.6 select_bitcast_fusion.1
  421.5 98.2 %all_to_all.15 = f32[2,16,16,896]{3,2,0,1:T(8,128)} all-to-all(f32[2,16,16,896]{3,2,0,1:T(8,128)S(1)} %get-tuple-element.48), channel_id=1, replica_groups=mesh['dp'=16,'tensor'=16] {'tensor'}, dimensions={1} | all-to-all | bytes 3670016 | tf_op jit(solution)/shard_map/all_to_all | solution.py:67
  519.7 12.7 %all-to-all-start.2 = ((f32[2,16,16,896]{3,2,0,1:T(8,128)}), f32[2,16,16,896]{3,2,0,1:T(8,128)}, u32[]{:S(2)}, u32[]{:S(2)}) async-start(f32[2,16,16,896]{3,2,0,1:T(8,128)} %get-tuple-element.47), calls=%async_computation.3 | async-start | bytes 3670016 | tf_op jit(solution)/shard_map/all_to_all | solution.py:68
  533.6 2.9 copy.81
  536.5 3.4 gather_fusion.3
  540.0 57.1 %all-to-all-done.2 = f32[2,16,16,896]{3,2,0,1:T(8,128)} async-done(((f32[2,16,16,896]{3,2,0,1:T(8,128)}), f32[2,16,16,896]{3,2,0,1:T(8,128)}, u32[]{:S(2)}, u32[]{:S(2)}) %all-to-all-start.2) | async-done | bytes 1835040 | tf_op jit(solution)/shard_map/all_to_all | solution.py:68
  597.0 2.9 copy.87
  599.9 3.4 gather_fusion.5
  603.3 2.5 select_bitcast_fusion
  607.4 2.5 copy.86
  616.0 184.2 %reduce-scatter.2.cloned.1.call-done = bf16[256,1792]{0,1:T(8,128)(2,1)} async-done(((bf16[4096,1792]{0,1:T(8,128)(2,1)}), bf16[256,1792]{0,1:T(8,128)(2,1)}) %reduce-scatter.2.cloned.1.call-update) | async-done | bytes 917520 | tf_op jit(solution)/shard_map/reduce_scatter | solution.py:98
  802.2 3.6 fusion.11
  807.2 2.7 copy.95
  809.9 2.6 pad_maximum_fusion.1
  812.5 2.8 copy.94
  (58 shorter events, 31.6 us)
Async XLA Ops:
  7.2 405.5 %copy-start = (f32[2,256,896]{2,1,0:T(8,128)S(1)}, f32[2,256,896]{2,1,0:T(8,128)}, u32[]{:S(2)}) copy-start(f32[2,256,896]{2,1,0:T(8,128)} %param.17) | copy-start | bytes 5505028
  11.0 12.9 %copy-start.10 = (s32[16]{0:T(128)S(1)}, s32[16]{0:T(128)}, u32[]{:S(2)}) copy-start(s32[16]{0:T(128)} %param.19) | copy-start | bytes 196
  13.3 35.1 %all-to-all-start = ((bf16[2,16,16,896]{3,2,0,1:T(8,128)(2,1)}), bf16[2,16,16,896]{3,2,0,1:T(8,128)(2,1)S(1)}, u32[]{:S(2)}, u32[]{:S(2)}) async-start(bf16[2,16,16,896]{3,2,0,1:T(8,128)(2,1)} %select_bitcast_fusion.5), calls=%async_computation | async-start | bytes 1835008 | tf_op jit(solution)/shard_map/all_to_all | solution.py:58
  23.8 190.1 %all-gather.3.cloned.1.call-start = ((), (), s32[]{:S(2)}) async-start(), calls=%async_computation.4 | async-start | bytes 7798784 | tf_op jit(solution)/shard_map/all_gather | solution.py:75
  52.4 326.4 %all-gather.5.cloned.1.call-start = ((), (), s32[]{:S(2)}) async-start(), calls=%async_computation.5 | async-start | bytes 7798784 | tf_op jit(solution)/shard_map/all_gather | solution.py:74
  53.1 747.1 %reduce-scatter.2.cloned.1.call-start = ((), (), s32[]{:S(2)}) async-start(), calls=%async_computation.6 | async-start | bytes 15597568 | tf_op jit(solution)/shard_map/reduce_scatter | solution.py:98
  387.7 7.5 copy-start.7
  395.1 2.1 copy-start.1
  519.7 12.7 %copy-start.3 = (bf16[1,16,16,896]{3,2,0,1:T(8,128)(2,1)S(1)}, bf16[1,16,16,896]{3,2,0,1:T(8,128)(2,1)}, u32[]{:S(2)}) copy-start(bf16[1,16,16,896]{3,2,0,1:T(8,128)(2,1)} %get-tuple-element.44) | copy-start | bytes 1376260
  519.7 12.9 %copy-start.2 = (bf16[1,16,16,896]{3,2,0,1:T(8,128)(2,1)S(1)}, bf16[1,16,16,896]{3,2,0,1:T(8,128)(2,1)}, u32[]{:S(2)}) copy-start(bf16[1,16,16,896]{3,2,0,1:T(8,128)(2,1)} %get-tuple-element.43) | copy-start | bytes 1376260
  519.7 77.3 %all-to-all-start.2 = ((f32[2,16,16,896]{3,2,0,1:T(8,128)}), f32[2,16,16,896]{3,2,0,1:T(8,128)}, u32[]{:S(2)}, u32[]{:S(2)}) async-start(f32[2,16,16,896]{3,2,0,1:T(8,128)} %get-tuple-element.47), calls=%async_computation.3 | async-start | bytes 3670016 | tf_op jit(solution)/shard_map/all_to_all | solution.py:68
  800.2 1.5 copy-start.4
  800.2 1.7 copy-start.5
  800.2 2.0 copy-start.6
  812.5 2.8 copy-start.9
  812.5 3.8 copy-start.8
Sparse Core Ops, SparseCore 0:
  52.5 161.3 all-gather.2
  216.3 162.4 all-gather.4
  412.8 387.4 reduce-scatter.1
where the time goes:
time: 831 us; the launch traced here: 824 us
  waiting for transfers between devices  583 us (70%)
  blocking collectives  98.2 us (12%)
  local copies, waits for them, and re-layouts  42 us (5%)
  other arithmetic  41.2 us (5%)
  starting transfers between devices  23.4 us (3%)
  matrix products  22.3 us (3%)
  between operations  13.9 us (2%)
    reduce_scatter x1, waiting for transfers between devices, per_device(): lax.psum_scatter(jnp.concatenate([jnp.einsum('rd,rf->df', cols_x, slope,...  184 us
    all_gather x1, waiting for transfers between devices, per_device(): down_piece = lax.all_gather(down_weight, 'dp', axis=0, tiled=True)  161 us
    all_gather x1, waiting for transfers between devices, per_device(): up_piece = lax.all_gather(up_weight, 'dp', axis=0, tiled=True)  156 us
    all_to_all x1, blocking collectives, per_device(): lax.all_to_all(first_out, 'tensor', split_axis=1, concat_axis=1, tiled=True)  98.2 us
    all_to_all x1, waiting for transfers between devices, per_device(): lax.all_to_all(second_out, 'tensor', split_axis=1, concat_axis=1, tiled=T...  57.1 us
    all_to_all x1, waiting for transfers between devices, per_device(): lax.all_to_all(outgoing, 'tensor', split_axis=1, concat_axis=1, tiled=True)  24.3 us
  transfers between devices with their start and end apart: 5, of which 5 were waited for; matrix products, arithmetic and copies ran while one was open for 5% of the time, Pallas kernels for 0%

commit v1 on v0

v1 whole, which is shorter than its diff:
```python
import jax
import jax.numpy as jnp
from jax import lax
from jax.experimental import pallas as pl
from jax.experimental.pallas import tpu as pltpu
from jax.sharding import PartitionSpec as P

beta_first = 0.9
beta_second = 0.95
adam_eps = 1e-08
rate = 0.005
step_count = 20

MESH = pl.DeviceIdType.MESH
BF = jnp.bfloat16
F32 = jnp.float32

N = 16
PIECE = 16
ROWS = 256
WIDTH = 896
QUART = 224
D = 4096
TOK = 1024
CHUNK = 1024
PART = 32


def wait_bytes(ref, sem):
    pltpu.make_async_copy(ref, ref, sem).wait()


def exchange(
    bd,
    rank,
    tok,
    cot,
    upk,
    dnk,
    fst,
    snd,
    momr,
    gout,
    X,
    stg,
    wst,
    wq,
    wr,
    mom,
    wall,
    acc,
    act,
    gp,
    relay,
    got,
    gsum,
    order,
    pick,
    loc,
    t1s,
    t1r,
    t2s,
    t2r,
    t3s,
    t3r,
    wqs,
    wqr,
    ags,
    agr,
    rss,
    rsr,
    ms,
    mr,
    zs,
    zr,
):
    dp = lax.axis_index("dp")
    tg = lax.axis_index("tensor")
    y, zl = dp // 4, dp % 4
    zh, x, c = tg // 8, (tg // 2) % 4, tg % 2
    z = zh * 4 + zl
    e = x * 2 + c

    def at(dy=0, dz=0, dx=0, dc=0):
        ny, nz, nx, nc = (y + dy + 4) % 4, (z + dz + 8) % 8, (x + dx + 4) % 4, (c + dc) % 2
        return (ny * 4 + nz % 4, (nz // 4) * 8 + nx * 2 + nc)

    def send(src, dst, ssem, rsem, dev):
        pltpu.make_async_remote_copy(
            src_ref=src,
            dst_ref=dst,
            send_sem=ssem,
            recv_sem=rsem,
            device_id=dev,
            device_id_type=MESH,
        ).start()

    def rows(z_, e_, half=None):
        if half is None:
            return X.at[:, pl.ds(pl.multiple_of(z_ * 256 + e_ * PART, PART), PART), :]
        return X.at[:, pl.ds(pl.multiple_of(z_ * 256 + e_ * PART + half * 16, 16), 16), :]

    own = pl.ds(pl.multiple_of(zl * 256, 256), 256)
    copies = [
        pltpu.make_async_copy(tok, X.at[0, own, :], loc.at[0]),
        pltpu.make_async_copy(cot, X.at[1, own, :], loc.at[1]),
        pltpu.make_async_copy(upk, wst.at[0], loc.at[2]),
        pltpu.make_async_copy(dnk, wst.at[1], loc.at[3]),
        pltpu.make_async_copy(fst, stg.at[pl.ds(0, 2)], loc.at[4]),
        pltpu.make_async_copy(snd, stg.at[pl.ds(2, 2)], loc.at[5]),
    ]
    for copy in copies:
        copy.start()

    copies[0].wait()
    copies[1].wait()
    send(rows(zl, e), rows(zl, e), t1s.at[0], t1r.at[0], at(dz=1))
    send(rows(zl, e), rows(zl, e), t1s.at[1], t1r.at[1], at(dz=-1))
    send(rows(zl, e, 0), rows(zl, e, 0), t1s.at[2], t1r.at[2], at(dz=2))
    send(rows(zl, e, 1), rows(zl, e, 1), t1s.at[3], t1r.at[3], at(dz=-2))

    line = lax.broadcasted_iota(jnp.int32, (ROWS, ROWS), 0)
    lane = lax.broadcasted_iota(jnp.int32, (ROWS, ROWS), 1)
    to_block = jnp.zeros((ROWS, ROWS), jnp.int32)
    from_block = jnp.zeros((ROWS, ROWS), jnp.int32)
    for k in range(N):
        here = (lane >> 4) == k
        to_block = jnp.where(here, bd[tg, k], to_block)
        from_block = jnp.where(here, (rank[k] + tg) & 15, from_block)
    within = (line & 15) == (lane & 15)
    order[...] = jnp.where(within & (to_block == (line >> 4)), 1.0, 0.0).astype(BF)
    pick[...] = jnp.where(within & (from_block == (line >> 4)), 1.0, 0.0).astype(BF)

    copies[2].wait()
    copies[3].wait()
    for m in range(2):
        sorted_rows = jnp.dot(order[...], wst[m], preferred_element_type=F32).astype(BF)
        mom[:, 4 + m] = sorted_rows.reshape(N, PIECE, WIDTH)
        wide = jnp.concatenate([sorted_rows, jnp.zeros((ROWS, 128), BF)], axis=1)
        for q in range(4):
            wq[:, q, m * PIECE : (m + 1) * PIECE, :] = wide[:, q * QUART : q * QUART + 256].reshape(
                N, PIECE, 256
            )

    me = z * 8 + e

    def send_weight(k, _):
        to = (me + k) % 64
        nz, nx, nc = to // 8, (to // 2) % 4, to % 2
        nt, nq = (nz // 4) * 8 + nx * 2 + nc, nz % 4
        send(wq.at[nt, nq], wr.at[zl * N + tg], wqs, wqr, (y * 4 + nq, nt))
        return 0

    lax.fori_loop(1, 64, send_weight, 0)
    own_block = pltpu.make_async_copy(wq.at[tg, zl], wr.at[zl * N + tg], loc.at[6])
    own_block.start()

    copies[4].wait()
    copies[5].wait()

    for k in range(4):
        sorted_rows = jnp.dot(order[...], stg[k].astype(BF), preferred_element_type=F32)
        mom[:, k] = sorted_rows.astype(BF).reshape(N, PIECE, WIDTH)

    came = [(zl + 3) % 4, (zl + 1) % 4, (zl + 2) % 4]
    for p in range(3):
        if p < 2:
            wait_bytes(rows(came[p], e), t1r.at[p])
        else:
            wait_bytes(rows(came[p], e, 0), t1r.at[2])
            wait_bytes(rows(came[p], e, 1), t1r.at[3])
        piece = rows(came[p], e)
        send(piece, piece, t2s.at[p, 0], t2r.at[p, 0], at(dx=1))
        send(piece, piece, t2s.at[p, 1], t2r.at[p, 1], at(dx=-1))
        send(piece, piece, t3s.at[p, 0], t3r.at[p, 0], at(dc=1))

    wait_bytes(wr.at[pl.ds(0, 63)], wqr)
    own_block.wait()

    def unpack(k, _):
        for m in range(2):
            block = wr[pl.ds(k * N, N), m * PIECE : (m + 1) * PIECE, :].reshape(ROWS, 256)
            turned = lax.dot_general(
                block, pick[...], (((0,), (1,)), ((), ())), preferred_element_type=F32
            )
            wall[y, m, :, pl.ds(pl.multiple_of(k * 256, 256), 256)] = turned[:QUART].astype(BF)
        return 0

    lax.fori_loop(0, 4, unpack, 0)
    send(wall.at[y], wall.at[y], ags.at[0], agr.at[0], at(dy=1))
    send(wall.at[y], wall.at[y], ags.at[1], agr.at[1], at(dy=-1))

    def send_moments(k, _):
        to = (tg + k) % N
        send(mom.at[to], momr.at[tg], ms, mr, (dp, to))
        return 0

    lax.fori_loop(1, N, send_moments, 0)
    own_moments = pltpu.make_async_copy(mom.at[tg], momr.at[tg], loc.at[7])
    own_moments.start()

    left, right, far = (x + 3) % 4 * 2 + c, (x + 1) % 4 * 2 + c, (x + 2) % 4 * 2 + c
    yl, yr, yf = (y + 3) % 4, (y + 1) % 4, (y + 2) % 4

    def pass_x(p):
        piece = rows(came[p], left)
        wait_bytes(piece, t2r.at[p, 0])
        half = rows(came[p], left, 0)
        send(half, half, t2s.at[p, 2], t2r.at[p, 2], at(dx=1))
        send(piece, piece, t3s.at[p, 1], t3r.at[p, 1], at(dc=1))
        piece = rows(came[p], right)
        wait_bytes(piece, t2r.at[p, 1])
        half = rows(came[p], right, 1)
        send(half, half, t2s.at[p, 3], t2r.at[p, 3], at(dx=-1))
        send(piece, piece, t3s.at[p, 2], t3r.at[p, 2], at(dc=1))

    pass_x(0)
    pass_x(1)
    wait_bytes(wall.at[yl], agr.at[0])
    send(wall.at[yl, 0], wall.at[yl, 0], ags.at[2], agr.at[2], at(dy=1))
    wait_bytes(wall.at[yr], agr.at[1])
    send(wall.at[yr, 1], wall.at[yr, 1], ags.at[3], agr.at[3], at(dy=-1))
    pass_x(2)
    for p in range(3):
        wait_bytes(rows(came[p], far, 0), t2r.at[p, 2])
        wait_bytes(rows(came[p], far, 1), t2r.at[p, 3])
        piece = rows(came[p], far)
        send(piece, piece, t3s.at[p, 3], t3r.at[p, 3], at(dc=1))
    for p in range(3):
        for k, dx in enumerate((0, 3, 1, 2)):
            wait_bytes(rows(came[p], (x + dx) % 4 * 2 + (1 - c)), t3r.at[p, k])
    wait_bytes(wall.at[yf, 0], agr.at[2])
    wait_bytes(wall.at[yf, 1], agr.at[3])

    acc[...] = jnp.zeros_like(acc)

    def forward(i, _):
        ny, k = i // 4, i % 4
        cols = pl.ds(pl.multiple_of(i * 256, 256), 256)
        part = pl.ds(pl.multiple_of(k * 256, 256), 256)
        for m in range(2):
            product = lax.dot_general(
                wall[ny, m, :, part],
                X[m, :, cols],
                (((1,), (1,)), ((), ())),
                preferred_element_type=F32,
            )
            acc[m] += product.astype(BF).astype(F32)
        return 0

    lax.fori_loop(0, N, forward, 0)

    def activate(i, _):
        cols = pl.ds(pl.multiple_of(i * 256, 256), 256)
        pre, back = acc[0, :, cols], acc[1, :, cols]
        sigma = jax.nn.sigmoid(pre)
        act[1, :, cols] = (pre * sigma).astype(BF)
        act[0, :, cols] = (back * sigma * (1.0 + pre * (1.0 - sigma))).astype(BF)
        return 0

    lax.fori_loop(0, 4, activate, 0)

    def gradient(ny):
        def step(i, _):
            cols = pl.ds(pl.multiple_of(ny * CHUNK + i * 256, 256), 256)
            part = pl.ds(pl.multiple_of(i * 256, 256), 256)
            for m in range(2):
                gp[ny, m, :, part] = jnp.dot(
                    act[m], X[m, :, cols], preferred_element_type=F32
                ).astype(BF)
            return 0

        lax.fori_loop(0, 4, step, 0)

    gradient(yf)
    send(gp.at[yf, 0], relay.at[0], rss.at[0], rsr.at[0], at(dy=1))
    send(gp.at[yf, 1], relay.at[1], rss.at[1], rsr.at[1], at(dy=-1))
    gradient(yr)
    send(gp.at[yr, 1], got.at[0, 1], rss.at[2], rsr.at[2], at(dy=1))
    gradient(yl)
    send(gp.at[yl, 0], got.at[1, 0], rss.at[3], rsr.at[3], at(dy=-1))
    gradient(y)
    wait_bytes(relay.at[0], rsr.at[0])
    gp[yr, 0] = (gp[yr, 0].astype(F32) + relay[0].astype(F32)).astype(BF)
    send(gp.at[yr, 0], got.at[0, 0], rss.at[4], rsr.at[4], at(dy=1))
    wait_bytes(relay.at[1], rsr.at[1])
    gp[yl, 1] = (gp[yl, 1].astype(F32) + relay[1].astype(F32)).astype(BF)
    send(gp.at[yl, 1], got.at[1, 1], rss.at[5], rsr.at[5], at(dy=-1))
    wait_bytes(got.at[0, 1], rsr.at[2])
    wait_bytes(got.at[1, 0], rsr.at[3])
    wait_bytes(got.at[0, 0], rsr.at[4])
    wait_bytes(got.at[1, 1], rsr.at[5])
    for m in range(2):
        gsum[m] = (
            gp[y, m].astype(F32) + got[0, m].astype(F32) + got[1, m].astype(F32)
        ).astype(BF)

    for k in range(1, 4):
        nq = (zl + k) % 4
        part = gsum.at[:, :, pl.ds(pl.multiple_of(nq * 256, 256), 256)]
        send(part, gout.at[zl], zs.at[k - 1], zr.at[k - 1], (y * 4 + nq, tg))
    own_part = pltpu.make_async_copy(
        gsum.at[:, :, pl.ds(pl.multiple_of(zl * 256, 256), 256)], gout.at[zl], loc.at[8]
    )
    own_part.start()

    wait_bytes(rows(zl, e), t1s.at[0])
    wait_bytes(rows(zl, e), t1s.at[1])
    wait_bytes(rows(zl, e, 0), t1s.at[2])
    wait_bytes(rows(zl, e, 1), t1s.at[3])
    for p in range(3):
        for k in range(4):
            wait_bytes(rows(zl, e, None if k < 2 else 0), t2s.at[p, k])
            wait_bytes(rows(zl, e), t3s.at[p, k])
    wait_bytes(wr.at[pl.ds(0, 63)], wqs)
    for k in range(2):
        wait_bytes(wall.at[y], ags.at[k])
        wait_bytes(wall.at[y, 0], ags.at[2 + k])
    for k in range(6):
        wait_bytes(gp.at[y, 0], rss.at[k])
    wait_bytes(mom.at[pl.ds(0, 15)], ms)
    wait_bytes(momr.at[pl.ds(0, 15)], mr)
    own_moments.wait()
    for k in range(3):
        wait_bytes(gout.at[k], zs.at[k])
        wait_bytes(gout.at[(zl + 3 - k) % 4], zr.at[k])
    own_part.wait()


def update(rank, momr, gin, new_up, new_dn, new_first, new_second, grad):
    step = pl.program_id(0)
    tg = lax.axis_index("tensor")

    @pl.when(step == 0)
    def _():
        for m in range(2):
            for q in range(2):
                lanes = pl.ds(q * 128, 128)
                tall = jnp.concatenate([gin[k, m, :, lanes].astype(F32) for k in range(4)], axis=0)
                grad[m, lanes, :] = tall.T

    for half in range(2):
        r = step * 2 + half
        src = jnp.int32(0)
        for k in range(N):
            src = src + jnp.where((rank[k] + tg) % N == r, k, 0)
        at_row = pl.ds(pl.multiple_of(r * PIECE, PIECE), PIECE)
        out_row = pl.ds(half * PIECE, PIECE)
        for m in range(2):
            g = grad[m, at_row, :]
            first = beta_first * momr[src, m].astype(F32) + (1.0 - beta_first) * g
            second = beta_second * momr[src, 2 + m].astype(F32) + (1.0 - beta_second) * g * g
            first_hat = first / (1.0 - beta_first**step_count)
            second_hat = second / (1.0 - beta_second**step_count)
            new = momr[src, 4 + m].astype(F32) - rate * first_hat / (jnp.sqrt(second_hat) + adam_eps)
            new_first[m, out_row, :] = first
            new_second[m, out_row, :] = second
            (new_up, new_dn)[m][out_row, :] = new.astype(BF)


def per_device(tok, cot, upk, dnk, fst, snd, bd, rank):
    anywhere = pl.BlockSpec(memory_space=pl.ANY)
    scalar = pl.BlockSpec(memory_space=pltpu.SMEM)
    dma = pltpu.SemaphoreType.DMA
    momr, gout = pl.pallas_call(
        exchange,
        out_shape=(
            jax.ShapeDtypeStruct((N, 6, PIECE, WIDTH), BF),
            jax.ShapeDtypeStruct((4, 2, QUART, 256), BF),
        ),
        in_specs=[scalar, scalar] + [anywhere] * 6,
        out_specs=(anywhere, anywhere),
        scratch_shapes=[
            pltpu.VMEM((2, TOK, D), BF),
            pltpu.VMEM((4, ROWS, WIDTH), F32),
            pltpu.VMEM((2, ROWS, WIDTH), BF),
            pltpu.VMEM((N, 4, 32, 256), BF),
            pltpu.VMEM((64, 32, 256), BF),
            pltpu.VMEM((N, 6, PIECE, WIDTH), BF),
            pltpu.VMEM((4, 2, QUART, CHUNK), BF),
            pltpu.VMEM((2, QUART, TOK), F32),
            pltpu.VMEM((2, QUART, TOK), BF),
            pltpu.VMEM((4, 2, QUART, CHUNK), BF),
            pltpu.VMEM((2, QUART, CHUNK), BF),
            pltpu.VMEM((2, 2, QUART, CHUNK), BF),
            pltpu.VMEM((2, QUART, CHUNK), BF),
            pltpu.VMEM((ROWS, ROWS), BF),
            pltpu.VMEM((ROWS, ROWS), BF),
            dma((9,)),
            dma((4,)),
            dma((4,)),
            dma((3, 4)),
            dma((3, 4)),
            dma((3, 4)),
            dma((3, 4)),
            dma,
            dma,
            dma((4,)),
            dma((4,)),
            dma((6,)),
            dma((6,)),
            dma,
            dma,
            dma((3,)),
            dma((3,)),
        ],
        compiler_params=pltpu.CompilerParams(
            has_side_effects=True, vmem_limit_bytes=60 * 2**20
        ),
        cost_estimate=pl.CostEstimate(
            flops=7_600_000_000, bytes_accessed=20_000_000, transcendentals=500_000
        ),
        name="exchange",
    )(bd, rank, tok, cot, upk, dnk, fst, snd)

    whole = pl.BlockSpec((N, 6, PIECE, WIDTH), lambda i: (0, 0, 0, 0))
    flat = pl.BlockSpec((32, WIDTH), lambda i: (i, 0))
    pair = pl.BlockSpec((2, 32, WIDTH), lambda i: (0, i, 0))
    return pl.pallas_call(
        update,
        grid=(8,),
        out_shape=(
            jax.ShapeDtypeStruct((ROWS, WIDTH), BF),
            jax.ShapeDtypeStruct((ROWS, WIDTH), BF),
            jax.ShapeDtypeStruct((2, ROWS, WIDTH), F32),
            jax.ShapeDtypeStruct((2, ROWS, WIDTH), F32),
        ),
        in_specs=[scalar, whole, pl.BlockSpec((4, 2, QUART, 256), lambda i: (0, 0, 0, 0))],
        out_specs=(flat, flat, pair, pair),
        scratch_shapes=[pltpu.VMEM((2, ROWS, WIDTH), F32)],
        compiler_params=pltpu.CompilerParams(vmem_limit_bytes=32 * 2**20),
        cost_estimate=pl.CostEstimate(
            flops=10_000_000, bytes_accessed=13_000_000, transcendentals=500_000
        ),
        name="update",
    )(rank, momr, gout)


def solution(mesh):
    in_specs = (
        P("dp", None),
        P("dp", None),
        P("dp", "tensor"),
        P("dp", "tensor"),
        P(None, "dp", "tensor"),
        P(None, "dp", "tensor"),
        P(),
        P(),
    )
    out_specs = (
        P("dp", "tensor"),
        P("dp", "tensor"),
        P(None, "dp", "tensor"),
        P(None, "dp", "tensor"),
    )
    return jax.shard_map(
        per_device, mesh=mesh, in_specs=in_specs, out_specs=out_specs, check_vma=False
    )
```

time: 831 us -> 203 us (0.24)
  waiting for transfers between devices: 583 us -> 0 us
  Pallas kernels: 0 us -> 196 us
  blocking collectives: 98.2 us -> 0 us
  other arithmetic: 41.2 us -> 0 us
  local copies, waits for them, and re-layouts: 42 us -> 2.95 us
  starting transfers between devices: 23.4 us -> 0 us
  matrix products: 22.3 us -> 0 us
  between operations: 13.9 us -> 0.67 us
    all_gather x2 -> x0, waiting for transfers between devices: 317 us -> none  [the longest x1 161 us: per_device(): down_piece = lax.all_gather(down_weight, 'dp', axis=0, tiled=True)]
    pallas_call x0 -> x2, Pallas kernels: none -> 196 us  [the longest x1 191 us: per_device(): pl.pallas_call(exchange, out_shape=(jax.ShapeDtypeStruct((N, 6, PIECE, WI...]
    reduce_scatter x1 -> x0, waiting for transfers between devices: 184 us -> none  [per_device(): lax.psum_scatter(jnp.concatenate([jnp.einsum('rd,rf->df', cols_x, slope,...]
    all_to_all x1 -> x0, blocking collectives: 98.2 us -> none  [per_device(): lax.all_to_all(first_out, 'tensor', split_axis=1, concat_axis=1, tiled=True)]
    all_to_all x2 -> x0, waiting for transfers between devices: 81.3 us -> none  [the longest x1 57.1 us: per_device(): lax.all_to_all(second_out, 'tensor', split_axis=1, concat_axis=1, tiled=T...]
    all_to_all x2 -> x0, starting transfers between devices: 23.2 us -> none  [the longest x1 12.7 us: per_device(): lax.all_to_all(second_out, 'tensor', split_axis=1, concat_axis=1, tiled=T...]
    dot_general x4 -> x0, matrix products: 22.3 us -> none  [the longest x1 8.98 us: per_device(): jnp.einsum('rkd,kdf->krf', cols_dy, down_piece.reshape(count, rows_dev, w...]
    gather x6 -> x0, local copies, waits for them, and re-layouts: 15.5 us -> none  [the longest x1 3.43 us: per_device(): jnp.take(first_in, recv_pick, axis=1).reshape(2, rows_dev, width)]
  transfers between devices with their start and end apart: 5 -> 0, of which waited for: 5 -> 0; matrix products, arithmetic and copies ran while one was open for 5% -> 0% of each run, Pallas kernels for 0% -> 0%
where the time goes in v1:
time: 203 us; the launch traced here: 200 us
  Pallas kernels  196 us (97%)
  local copies, waits for them, and re-layouts  2.95 us (1%)
    pallas_call x1, Pallas kernels, per_device(): pl.pallas_call(exchange, out_shape=(jax.ShapeDtypeStruct((N, 6, PIECE, WI...  191 us
    pallas_call x1, Pallas kernels, per_device(): pl.pallas_call(update, grid=(8,), out_shape=(jax.ShapeDtypeStruct((ROWS,...  5.35 us

profile of v1, /device:TPU:34, one launch (start us, length us, event | category | flops | bytes accessed | tf_op | source)
XLA Modules:
  0.0 200.1 jit_solution(3681475099796166171)
XLA Ops:
  0.6 0.0 copy-start.2
  0.6 191.1 %exchange.1 = (bf16[16,6,16,896]{3,2,1,0:T(8,128)(2,1)}, bf16[4,2,224,256]{3,2,1,0:T(8,128)(2,1)}) custom-call(s32[16,16]{1,0:T(8,128)} %bd.1, s32[16]{0:T(128)} %rank.3, bf16[256,4096]{1,0:T(8,128)(2,1)} %tok.1, bf16[256,4096]{1,0:T(8,128)(2,1)} %cot.1, bf16[256,896]{1,0:T(8,128)(2,1)} %upk.1, bf16[256,896]{1,0:T(8,128)(2,1)} %dnk.1, f32[2,256,896]{2,1,0:T(8,128)} %fst.1, ...), custom_call_target="tpu_custom_call" | custom-call | flops 7600000000 | bytes 20000000 | tf_op jit(solution)/shard_map/exchange/pallas_call | solution.py:365
  191.7 0.0 copy-done.2
  191.7 0.0 copy-start
  191.8 1.8 copy-done
  193.5 0.0 copy-start.1
  193.5 1.2 copy-done.1
  194.7 5.4 %update.1 = (bf16[256,896]{1,0:T(8,128)(2,1)}, bf16[256,896]{1,0:T(8,128)(2,1)}, f32[2,256,896]{2,1,0:T(8,128)}, f32[2,256,896]{2,1,0:T(8,128)}) custom-call(s32[16]{0:T(128)S(1)} %copy-done.2, bf16[16,6,16,896]{3,2,1,0:T(8,128)(2,1)S(1)} %copy-done, bf16[4,2,224,256]{3,2,1,0:T(8,128)(2,1)S(1)} %copy-done.1), custom_call_target="tpu_custom_call" | custom-call | flops 10000000 | bytes 13000000 | tf_op jit(solution)/shard_map/update/pallas_call | solution.py:419
Async XLA Ops:
  0.6 191.1 %copy-start.2 = (s32[16]{0:T(128)S(1)}, s32[16]{0:T(128)}, u32[]{:S(2)}) copy-start(s32[16]{0:T(128)} %rank.3) | copy-start | bytes 196
  191.7 1.8 copy-start
  193.5 1.2 copy-start.1

commit v2 on v1

v2 whole, which is shorter than its diff:
```python
import jax
import jax.numpy as jnp
from jax import lax
from jax.experimental import pallas as pl
from jax.experimental.pallas import tpu as pltpu
from jax.sharding import PartitionSpec as P

beta_first = 0.9
beta_second = 0.95
adam_eps = 1e-08
rate = 0.005
step_count = 20

MESH = pl.DeviceIdType.MESH
BF = jnp.bfloat16
F32 = jnp.float32

N = 16
PIECE = 16
ROWS = 256
WIDTH = 896
QUART = 224
HALF = 112
D = 4096
TOK = 1024
CHUNK = 1024
PART = 32


def wait_bytes(ref, sem):
    pltpu.make_async_copy(ref, ref, sem).wait()


def exchange(
    bd,
    rank,
    tok,
    cot,
    upk,
    dnk,
    fst,
    snd,
    momr,
    gout,
    X,
    stg,
    wst,
    wq,
    wr,
    mom,
    wall,
    acc,
    act,
    gp,
    relay,
    got,
    gsum,
    order,
    pick,
    row_in,
    pair_in,
    loc,
    t1s,
    t1r,
    t2s,
    t2r,
    t3s,
    t3r,
    wqs,
    wqr,
    ags,
    agr,
    rss,
    rsr,
    ms,
    mr,
    zs,
    zr,
):
    dp = lax.axis_index("dp")
    tg = lax.axis_index("tensor")
    y, zl = dp // 4, dp % 4
    zh, x, c = tg // 8, (tg // 2) % 4, tg % 2
    z = zh * 4 + zl
    e = x * 2 + c

    def at(dy=0, dz=0, dx=0, dc=0):
        ny, nz, nx, nc = (y + dy + 4) % 4, (z + dz + 8) % 8, (x + dx + 4) % 4, (c + dc) % 2
        return (ny * 4 + nz % 4, (nz // 4) * 8 + nx * 2 + nc)

    def send(src, dst, ssem, rsem, dev):
        pltpu.make_async_remote_copy(
            src_ref=src,
            dst_ref=dst,
            send_sem=ssem,
            recv_sem=rsem,
            device_id=dev,
            device_id_type=MESH,
        ).start()

    def rows(z_, e_, half=None):
        if half is None:
            return X.at[:, pl.ds(pl.multiple_of(z_ * 256 + e_ * PART, PART), PART), :]
        return X.at[:, pl.ds(pl.multiple_of(z_ * 256 + e_ * PART + half * 16, 16), 16), :]

    own = pl.ds(pl.multiple_of(zl * 256, 256), 256)
    copies = [
        pltpu.make_async_copy(tok, X.at[0, own, :], loc.at[0]),
        pltpu.make_async_copy(cot, X.at[1, own, :], loc.at[1]),
        pltpu.make_async_copy(upk, wst.at[0], loc.at[2]),
        pltpu.make_async_copy(dnk, wst.at[1], loc.at[3]),
        pltpu.make_async_copy(fst, stg.at[pl.ds(0, 2)], loc.at[4]),
        pltpu.make_async_copy(snd, stg.at[pl.ds(2, 2)], loc.at[5]),
    ]
    for copy in copies:
        copy.start()

    barrier = pltpu.get_barrier_semaphore()

    def greet(sem, dev):
        pl.semaphore_signal(sem, inc=1, device_id=dev, device_id_type=MESH)

    for k in range(1, 8):
        greet(barrier, at(dz=k))
    for k in range(1, 4):
        greet(barrier, at(dx=k))
    greet(barrier, at(dc=1))
    greet(barrier, at(dy=1))
    greet(barrier, at(dy=-1))
    pl.semaphore_wait(barrier, 13)
    for k in range(1, 4):
        greet(row_in, at(dx=k))

    copies[0].wait()
    copies[1].wait()
    for k in range(2):
        send(rows(zl, e, k), rows(zl, e, k), t1s.at[k], t1r.at[k], at(dz=1))
        send(rows(zl, e, 1 - k), rows(zl, e, 1 - k), t1s.at[2 + k], t1r.at[2 + k], at(dz=-1))

    line = lax.broadcasted_iota(jnp.int32, (ROWS, ROWS), 0)
    lane = lax.broadcasted_iota(jnp.int32, (ROWS, ROWS), 1)
    to_block = jnp.zeros((ROWS, ROWS), jnp.int32)
    from_block = jnp.zeros((ROWS, ROWS), jnp.int32)
    for k in range(N):
        here = (lane >> 4) == k
        to_block = jnp.where(here, bd[tg, k], to_block)
        from_block = jnp.where(here, (rank[k] + tg) & 15, from_block)
    within = (line & 15) == (lane & 15)
    order[...] = jnp.where(within & (to_block == (line >> 4)), 1.0, 0.0).astype(BF)
    pick[...] = jnp.where(within & (from_block == (line >> 4)), 1.0, 0.0).astype(BF)

    copies[2].wait()
    copies[3].wait()
    for m in range(2):
        sorted_rows = jnp.dot(order[...], wst[m], preferred_element_type=F32).astype(BF)
        mom[:, 4 + m] = sorted_rows.reshape(N, PIECE, WIDTH)
        wide = jnp.concatenate([sorted_rows, jnp.zeros((ROWS, 128), BF)], axis=1)
        for q in range(4):
            for h in range(2):
                first = q * QUART + h * HALF
                wq[:, q, h, m * PIECE : (m + 1) * PIECE, :] = wide[:, first : first + 128].reshape(
                    N, PIECE, 128
                )

    pl.semaphore_wait(row_in, 3)
    greet(pair_in, at(dc=1))

    copies[4].wait()
    copies[5].wait()
    for k in range(4):
        sorted_rows = jnp.dot(order[...], stg[k].astype(BF), preferred_element_type=F32)
        mom[:, k] = sorted_rows.astype(BF).reshape(N, PIECE, WIDTH)

    def send_moments(dzh, dx, dc):
        to = (zh + dzh) % 2 * 8 + (x + dx) % 4 * 2 + (c + dc) % 2
        send(mom.at[to], momr.at[tg], ms, mr, (dp, to))

    pl.semaphore_wait(pair_in, 1)

    def same_half(k, _):
        send_moments(0, k // 2, k % 2)
        return 0

    lax.fori_loop(1, 8, same_half, 0)
    own_moments = pltpu.make_async_copy(mom.at[tg], momr.at[tg], loc.at[7])
    own_moments.start()

    came = [(zl + 3) % 4, (zl + 1) % 4, (zl + 2) % 4]

    def spread(p, k):
        half = rows(came[p], e, k)
        send(half, half, t2s.at[p, k], t2r.at[p, k], at(dx=1))
        send(half, half, t2s.at[p, 2 + k], t2r.at[p, 2 + k], at(dx=-1))

    def spread_core(p):
        piece = rows(came[p], e)
        send(piece, piece, t3s.at[p, 0], t3r.at[p, 0], at(dc=1))

    half = rows(came[0], e, 0)
    wait_bytes(half, t1r.at[0])
    send(half, half, t1s.at[4], t1r.at[4], at(dz=1))
    spread(0, 0)
    half = rows(came[1], e, 1)
    wait_bytes(half, t1r.at[2])
    send(half, half, t1s.at[5], t1r.at[5], at(dz=-1))
    spread(1, 1)
    wait_bytes(rows(came[0], e, 1), t1r.at[1])
    spread(0, 1)
    wait_bytes(rows(came[1], e, 0), t1r.at[3])
    spread(1, 0)

    me = z * 8 + e

    def send_weights(h):
        def step(k, _):
            to = (me + k) % 64
            nz, nx, nc = to // 8, (to // 2) % 4, to % 2
            nt, nq = (nz // 4) * 8 + nx * 2 + nc, nz % 4
            send(wq.at[nt, nq, h], wr.at[h, zl * N + tg], wqs.at[h], wqr.at[h], (y * 4 + nq, nt))
            return 0

        lax.fori_loop(1, 64, step, 0)
        own_block = pltpu.make_async_copy(wq.at[tg, zl, h], wr.at[h, zl * N + tg], loc.at[10 + h])
        own_block.start()
        return own_block

    own_blocks = [send_weights(0), send_weights(1)]
    spread_core(0)
    spread_core(1)

    wait_bytes(rows(came[2], e, 0), t1r.at[4])
    spread(2, 0)
    wait_bytes(rows(came[2], e, 1), t1r.at[5])
    spread(2, 1)
    spread_core(2)

    for h in range(2):
        wait_bytes(wr.at[h, pl.ds(0, 63)], wqr.at[h])
        own_blocks[h].wait()

        def unpack(k, _, h=h):
            for m in range(2):
                block = wr[h, pl.ds(k * N, N), m * PIECE : (m + 1) * PIECE, :].reshape(ROWS, 128)
                turned = lax.dot_general(
                    block, pick[...], (((0,), (1,)), ((), ())), preferred_element_type=F32
                )
                part = pl.ds(pl.multiple_of(k * 256, 256), 256)
                wall[h, y, m, :, part] = turned[:HALF].astype(BF)
            return 0

        lax.fori_loop(0, 4, unpack, 0)
        send(wall.at[h, y], wall.at[h, y], ags.at[h, 0], agr.at[h, 0], at(dy=1))
        send(wall.at[h, y], wall.at[h, y], ags.at[h, 1], agr.at[h, 1], at(dy=-1))

    lax.fori_loop(0, 2, lambda k, _: (send_moments(1, 0, k), 0)[1], 0)

    def near_half(k, _):
        send_moments(1, 1 + k // 2 * 2, k % 2)
        return 0

    left, right, far = (x + 3) % 4 * 2 + c, (x + 1) % 4 * 2 + c, (x + 2) % 4 * 2 + c
    yl, yr, yf = (y + 3) % 4, (y + 1) % 4, (y + 2) % 4

    def pass_x(p):
        half = rows(came[p], left, 0)
        wait_bytes(half, t2r.at[p, 0])
        send(half, half, t2s.at[p, 4], t2r.at[p, 4], at(dx=1))
        half = rows(came[p], right, 1)
        wait_bytes(half, t2r.at[p, 3])
        send(half, half, t2s.at[p, 5], t2r.at[p, 5], at(dx=-1))
        wait_bytes(rows(came[p], left, 1), t2r.at[p, 1])
        piece = rows(came[p], left)
        send(piece, piece, t3s.at[p, 1], t3r.at[p, 1], at(dc=1))
        wait_bytes(rows(came[p], right, 0), t2r.at[p, 2])
        piece = rows(came[p], right)
        send(piece, piece, t3s.at[p, 2], t3r.at[p, 2], at(dc=1))

    def pass_y(h):
        wait_bytes(wall.at[h, yl], agr.at[h, 0])
        send(wall.at[h, yl, 0], wall.at[h, yl, 0], ags.at[h, 2], agr.at[h, 2], at(dy=1))
        wait_bytes(wall.at[h, yr], agr.at[h, 1])
        send(wall.at[h, yr, 1], wall.at[h, yr, 1], ags.at[h, 3], agr.at[h, 3], at(dy=-1))

    def end_x(p):
        wait_bytes(rows(came[p], far, 0), t2r.at[p, 4])
        wait_bytes(rows(came[p], far, 1), t2r.at[p, 5])
        piece = rows(came[p], far)
        send(piece, piece, t3s.at[p, 3], t3r.at[p, 3], at(dc=1))

    def end_tokens(p):
        for k, dx in enumerate((0, 3, 1, 2)):
            wait_bytes(rows(came[p], (x + dx) % 4 * 2 + (1 - c)), t3r.at[p, k])

    def end_y(h):
        wait_bytes(wall.at[h, yf, 0], agr.at[h, 2])
        wait_bytes(wall.at[h, yf, 1], agr.at[h, 3])

    def forward(nz):
        seen = pl.ds(pl.multiple_of(nz * 256, 256), 256)

        def step(ny, _):
            for m in range(2):
                total = jnp.zeros((QUART, 256), F32)
                for k in range(4):
                    cols = pl.ds(pl.multiple_of(ny * CHUNK + k * 256, 256), 256)
                    part = pl.ds(k * 256, 256)
                    weight = jnp.concatenate(
                        [wall[0, ny, m, :, part], wall[1, ny, m, :, part]], axis=0
                    )
                    product = lax.dot_general(
                        weight,
                        X[m, seen, cols],
                        (((1,), (1,)), ((), ())),
                        preferred_element_type=F32,
                    )
                    total += product.astype(BF).astype(F32)
                acc[m] += total
            return 0

        acc[...] = jnp.zeros_like(acc)
        lax.fori_loop(0, 4, step, 0)
        pre, back = acc[0], acc[1]
        sigma = jax.nn.sigmoid(pre)
        act[1, :, seen] = (pre * sigma).astype(BF)
        act[0, :, seen] = (back * sigma * (1.0 + pre * (1.0 - sigma))).astype(BF)

    upper, lower = pl.ds(0, HALF), pl.ds(HALF, HALF)

    def gradient(m, ny):
        def step(i, _):
            cols = pl.ds(pl.multiple_of(ny * CHUNK + i * 256, 256), 256)
            part = pl.ds(pl.multiple_of(i * 256, 256), 256)
            gp[m, ny, :, part] = jnp.dot(
                act[m], X[m, :, cols], preferred_element_type=F32
            ).astype(BF)
            return 0

        lax.fori_loop(0, 4, step, 0)

    def gradients(m):
        gradient(m, yf)
        send(gp.at[m, yf, upper], relay.at[m, 0], rss.at[m, 0], rsr.at[m, 0], at(dy=1))
        send(gp.at[m, yf, lower], relay.at[m, 1], rss.at[m, 1], rsr.at[m, 1], at(dy=-1))
        gradient(m, yr)
        send(gp.at[m, yr, lower], got.at[m, 0, lower], rss.at[m, 2], rsr.at[m, 2], at(dy=1))
        gradient(m, yl)
        send(gp.at[m, yl, upper], got.at[m, 1, upper], rss.at[m, 3], rsr.at[m, 3], at(dy=-1))
        gradient(m, y)

    def relays(m):
        wait_bytes(relay.at[m, 0], rsr.at[m, 0])
        gp[m, yr, upper] = (gp[m, yr, upper].astype(F32) + relay[m, 0].astype(F32)).astype(BF)
        send(gp.at[m, yr, upper], got.at[m, 0, upper], rss.at[m, 4], rsr.at[m, 4], at(dy=1))
        wait_bytes(relay.at[m, 1], rsr.at[m, 1])
        gp[m, yl, lower] = (gp[m, yl, lower].astype(F32) + relay[m, 1].astype(F32)).astype(BF)
        send(gp.at[m, yl, lower], got.at[m, 1, lower], rss.at[m, 5], rsr.at[m, 5], at(dy=-1))

    own_parts = []

    def finish(m):
        wait_bytes(got.at[m, 0, lower], rsr.at[m, 2])
        wait_bytes(got.at[m, 1, upper], rsr.at[m, 3])
        wait_bytes(got.at[m, 0, upper], rsr.at[m, 4])
        wait_bytes(got.at[m, 1, lower], rsr.at[m, 5])
        gsum[m] = (
            gp[m, y].astype(F32) + got[m, 0].astype(F32) + got[m, 1].astype(F32)
        ).astype(BF)
        for k in range(1, 4):
            nq = (zl + k) % 4
            part = gsum.at[m, :, pl.ds(pl.multiple_of(nq * 256, 256), 256)]
            send(part, gout.at[m, zl], zs.at[m, k - 1], zr.at[m, k - 1], (y * 4 + nq, tg))
        own_part = pltpu.make_async_copy(
            gsum.at[m, :, pl.ds(pl.multiple_of(zl * 256, 256), 256)], gout.at[m, zl], loc.at[8 + m]
        )
        own_part.start()
        own_parts.append(own_part)

    pass_x(0)
    pass_x(1)
    pass_y(0)
    pass_x(2)
    lax.fori_loop(0, 4, near_half, 0)
    pass_y(1)
    for p in range(3):
        end_x(p)
    lax.fori_loop(0, 2, lambda k, _: (send_moments(1, 2, k), 0)[1], 0)
    end_y(0)
    end_y(1)
    forward(zl)
    for p in range(3):
        end_tokens(p)
        forward(came[p])
    gradients(0)
    gradients(1)
    relays(0)
    relays(1)
    finish(0)
    finish(1)

    for k in range(6):
        wait_bytes(rows(zl, e, 0), t1s.at[k])
    for p in range(3):
        for k in range(6):
            wait_bytes(rows(zl, e, 0), t2s.at[p, k])
        for k in range(4):
            wait_bytes(rows(zl, e), t3s.at[p, k])
    for h in range(2):
        wait_bytes(wr.at[h, pl.ds(0, 63)], wqs.at[h])
    for h in range(2):
        for k in range(2):
            wait_bytes(wall.at[h, y], ags.at[h, k])
            wait_bytes(wall.at[h, y, 0], ags.at[h, 2 + k])
        for k in range(6):
            wait_bytes(gp.at[h, y, upper], rss.at[h, k])
        for k in range(3):
            wait_bytes(gout.at[h, k], zs.at[h, k])
            wait_bytes(gout.at[h, (zl + 3 - k) % 4], zr.at[h, k])
        own_parts[h].wait()
    wait_bytes(mom.at[pl.ds(0, 15)], ms)
    wait_bytes(momr.at[pl.ds(0, 15)], mr)
    own_moments.wait()


def update(rank, momr, gin, new_up, new_dn, new_first, new_second, grad):
    step = pl.program_id(0)
    tg = lax.axis_index("tensor")

    @pl.when(step == 0)
    def _():
        for m in range(2):
            for q in range(2):
                lanes = pl.ds(q * 128, 128)
                tall = jnp.concatenate([
                    gin[m, k, :, lanes].astype(F32) for k in range(4)
                ], axis=0)
                grad[m, lanes, :] = tall.T

    for half in range(2):
        r = step * 2 + half
        src = jnp.int32(0)
        for k in range(N):
            src = src + jnp.where((rank[k] + tg) % N == r, k, 0)
        at_row = pl.ds(pl.multiple_of(r * PIECE, PIECE), PIECE)
        out_row = pl.ds(half * PIECE, PIECE)
        for m in range(2):
            g = grad[m, at_row, :]
            first = beta_first * momr[src, m].astype(F32) + (1.0 - beta_first) * g
            second = beta_second * momr[src, 2 + m].astype(F32) + (1.0 - beta_second) * g * g
            first_hat = first / (1.0 - beta_first**step_count)
            second_hat = second / (1.0 - beta_second**step_count)
            new = momr[src, 4 + m].astype(F32) - rate * first_hat / (jnp.sqrt(second_hat) + adam_eps)
            new_first[m, out_row, :] = first
            new_second[m, out_row, :] = second
            (new_up, new_dn)[m][out_row, :] = new.astype(BF)


def per_device(tok, cot, upk, dnk, fst, snd, bd, rank):
    anywhere = pl.BlockSpec(memory_space=pl.ANY)
    scalar = pl.BlockSpec(memory_space=pltpu.SMEM)
    dma = pltpu.SemaphoreType.DMA
    momr, gout = pl.pallas_call(
        exchange,
        out_shape=(
            jax.ShapeDtypeStruct((N, 6, PIECE, WIDTH), BF),
            jax.ShapeDtypeStruct((2, 4, QUART, 256), BF),
        ),
        in_specs=[scalar, scalar] + [anywhere] * 6,
        out_specs=(anywhere, anywhere),
        scratch_shapes=[
            pltpu.VMEM((2, TOK, D), BF),
            pltpu.VMEM((4, ROWS, WIDTH), F32),
            pltpu.VMEM((2, ROWS, WIDTH), BF),
            pltpu.VMEM((N, 4, 2, 32, 128), BF),
            pltpu.VMEM((2, 64, 32, 128), BF),
            pltpu.VMEM((N, 6, PIECE, WIDTH), BF),
            pltpu.VMEM((2, 4, 2, HALF, CHUNK), BF),
            pltpu.VMEM((2, QUART, 256), F32),
            pltpu.VMEM((2, QUART, TOK), BF),
            pltpu.VMEM((2, 4, QUART, CHUNK), BF),
            pltpu.VMEM((2, 2, HALF, CHUNK), BF),
            pltpu.VMEM((2, 2, QUART, CHUNK), BF),
            pltpu.VMEM((2, QUART, CHUNK), BF),
            pltpu.VMEM((ROWS, ROWS), BF),
            pltpu.VMEM((ROWS, ROWS), BF),
            pltpu.SemaphoreType.REGULAR,
            pltpu.SemaphoreType.REGULAR,
            dma((12,)),
            dma((6,)),
            dma((6,)),
            dma((3, 6)),
            dma((3, 6)),
            dma((3, 4)),
            dma((3, 4)),
            dma((2,)),
            dma((2,)),
            dma((2, 4)),
            dma((2, 4)),
            dma((2, 6)),
            dma((2, 6)),
            dma,
            dma,
            dma((2, 3)),
            dma((2, 3)),
        ],
        compiler_params=pltpu.CompilerParams(
            has_side_effects=True, collective_id=0, vmem_limit_bytes=60 * 2**20
        ),
        cost_estimate=pl.CostEstimate(
            flops=7_600_000_000, bytes_accessed=20_000_000, transcendentals=500_000
        ),
        name="exchange",
    )(bd, rank, tok, cot, upk, dnk, fst, snd)

    whole = pl.BlockSpec((N, 6, PIECE, WIDTH), lambda i: (0, 0, 0, 0))
    flat = pl.BlockSpec((32, WIDTH), lambda i: (i, 0))
    pair = pl.BlockSpec((2, 32, WIDTH), lambda i: (0, i, 0))
    return pl.pallas_call(
        update,
        grid=(8,),
        out_shape=(
            jax.ShapeDtypeStruct((ROWS, WIDTH), BF),
            jax.ShapeDtypeStruct((ROWS, WIDTH), BF),
            jax.ShapeDtypeStruct((2, ROWS, WIDTH), F32),
            jax.ShapeDtypeStruct((2, ROWS, WIDTH), F32),
        ),
        in_specs=[scalar, whole, pl.BlockSpec((2, 4, QUART, 256), lambda i: (0,) * 4)],
        out_specs=(flat, flat, pair, pair),
        scratch_shapes=[pltpu.VMEM((2, ROWS, WIDTH), F32)],
        compiler_params=pltpu.CompilerParams(vmem_limit_bytes=32 * 2**20),
        cost_estimate=pl.CostEstimate(
            flops=10_000_000, bytes_accessed=13_000_000, transcendentals=500_000
        ),
        name="update",
    )(rank, momr, gout)


def solution(mesh):
    in_specs = (
        P("dp", None),
        P("dp", None),
        P("dp", "tensor"),
        P("dp", "tensor"),
        P(None, "dp", "tensor"),
        P(None, "dp", "tensor"),
        P(),
        P(),
    )
    out_specs = (
        P("dp", "tensor"),
        P("dp", "tensor"),
        P(None, "dp", "tensor"),
        P(None, "dp", "tensor"),
    )
    return jax.shard_map(
        per_device, mesh=mesh, in_specs=in_specs, out_specs=out_specs, check_vma=False
    )
```

time: 203 us -> 165 us (0.81)
  Pallas kernels: 196 us -> 159 us
    pallas_call x1, Pallas kernels: 191 us -> 154 us  [per_device(): pl.pallas_call(exchange, out_shape=(jax.ShapeDtypeStruct((N, 6, PIECE, WI...]
where the time goes in v2:
time: 165 us; the launch traced here: 163 us
  Pallas kernels  159 us (96%)
  local copies, waits for them, and re-layouts  2.95 us (2%)
    pallas_call x1, Pallas kernels, per_device(): pl.pallas_call(exchange, out_shape=(jax.ShapeDtypeStruct((N, 6, PIECE, WI...  154 us
    pallas_call x1, Pallas kernels, per_device(): pl.pallas_call(update, grid=(8,), out_shape=(jax.ShapeDtypeStruct((ROWS,...  5.35 us

profile of v2, /device:TPU:34, one launch (start us, length us, event | category | flops | bytes accessed | tf_op | source)
XLA Modules:
  0.0 162.7 jit_solution(14197048780352201917)
XLA Ops:
  0.6 0.0 copy-start.2
  0.6 153.7 %exchange.1 = (bf16[16,6,16,896]{3,2,1,0:T(8,128)(2,1)}, bf16[2,4,224,256]{3,2,1,0:T(8,128)(2,1)}) custom-call(s32[16,16]{1,0:T(8,128)} %bd.1, s32[16]{0:T(128)} %rank.3, bf16[256,4096]{1,0:T(8,128)(2,1)} %tok.1, bf16[256,4096]{1,0:T(8,128)(2,1)} %cot.1, bf16[256,896]{1,0:T(8,128)(2,1)} %upk.1, bf16[256,896]{1,0:T(8,128)(2,1)} %dnk.1, f32[2,256,896]{2,1,0:T(8,128)} %fst.1, ...), custom_call_target="tpu_custom_call" | custom-call | flops 7600000000 | bytes 20000000 | tf_op jit(solution)/shard_map/exchange/pallas_call | solution.py:461
  154.3 0.0 copy-done.2
  154.4 0.0 copy-start
  154.4 1.8 %copy-done = bf16[16,6,16,896]{3,2,1,0:T(8,128)(2,1)S(1)} copy-done((bf16[16,6,16,896]{3,2,1,0:T(8,128)(2,1)S(1)}, bf16[16,6,16,896]{3,2,1,0:T(8,128)(2,1)}, u32[]{:S(2)}) %copy-start) | copy-done | bytes 2752536
  156.1 0.0 copy-start.1
  156.1 1.2 copy-done.1
  157.3 5.4 %update.1 = (bf16[256,896]{1,0:T(8,128)(2,1)}, bf16[256,896]{1,0:T(8,128)(2,1)}, f32[2,256,896]{2,1,0:T(8,128)}, f32[2,256,896]{2,1,0:T(8,128)}) custom-call(s32[16]{0:T(128)S(1)} %copy-done.2, bf16[16,6,16,896]{3,2,1,0:T(8,128)(2,1)S(1)} %copy-done, bf16[2,4,224,256]{3,2,1,0:T(8,128)(2,1)S(1)} %copy-done.1), custom_call_target="tpu_custom_call" | custom-call | flops 10000000 | bytes 13000000 | tf_op jit(solution)/shard_map/update/pallas_call | solution.py:517
Async XLA Ops:
  0.6 153.7 %copy-start.2 = (s32[16]{0:T(128)S(1)}, s32[16]{0:T(128)}, u32[]{:S(2)}) copy-start(s32[16]{0:T(128)} %rank.3) | copy-start | bytes 196
  154.4 1.8 %copy-start = (bf16[16,6,16,896]{3,2,1,0:T(8,128)(2,1)S(1)}, bf16[16,6,16,896]{3,2,1,0:T(8,128)(2,1)}, u32[]{:S(2)}) copy-start(bf16[16,6,16,896]{3,2,1,0:T(8,128)(2,1)} %get-tuple-element.6.momr) | copy-start | bytes 8257540
  156.1 1.2 copy-start.1

commit v3 on v2

--- a/solution.py
+++ b/solution.py
@@ -164,26 +164,24 @@
 
     pl.semaphore_wait(row_in, 3)
     greet(pair_in, at(dc=1))
-
-    copies[4].wait()
-    copies[5].wait()
-    for k in range(4):
-        sorted_rows = jnp.dot(order[...], stg[k].astype(BF), preferred_element_type=F32)
-        mom[:, k] = sorted_rows.astype(BF).reshape(N, PIECE, WIDTH)
-
-    def send_moments(dzh, dx, dc):
-        to = (zh + dzh) % 2 * 8 + (x + dx) % 4 * 2 + (c + dc) % 2
-        send(mom.at[to], momr.at[tg], ms, mr, (dp, to))
-
     pl.semaphore_wait(pair_in, 1)
 
-    def same_half(k, _):
-        send_moments(0, k // 2, k % 2)
-        return 0
-
-    lax.fori_loop(1, 8, same_half, 0)
-    own_moments = pltpu.make_async_copy(mom.at[tg], momr.at[tg], loc.at[7])
-    own_moments.start()
+    me = z * 8 + e
+
+    def send_weights(h):
+        def step(k, _):
+            to = (me + k) % 64
+            nz, nx, nc = to // 8, (to // 2) % 4, to % 2
+            nt, nq = (nz // 4) * 8 + nx * 2 + nc, nz % 4
+            send(wq.at[nt, nq, h], wr.at[h, zl * N + tg], wqs.at[h], wqr.at[h], (y * 4 + nq, nt))
+            return 0
+
+        lax.fori_loop(1, 64, step, 0)
+        own_block = pltpu.make_async_copy(wq.at[tg, zl, h], wr.at[h, zl * N + tg], loc.at[10 + h])
+        own_block.start()
+        return own_block
+
+    own_blocks = [send_weights(0), send_weights(1)]
 
     came = [(zl + 3) % 4, (zl + 1) % 4, (zl + 2) % 4]
 
@@ -209,24 +207,22 @@
     wait_bytes(rows(came[1], e, 0), t1r.at[3])
     spread(1, 0)
 
-    me = z * 8 + e
-
-    def send_weights(h):
-        def step(k, _):
-            to = (me + k) % 64
-            nz, nx, nc = to // 8, (to // 2) % 4, to % 2
-            nt, nq = (nz // 4) * 8 + nx * 2 + nc, nz % 4
-            send(wq.at[nt, nq, h], wr.at[h, zl * N + tg], wqs.at[h], wqr.at[h], (y * 4 + nq, nt))
-            return 0
-
-        lax.fori_loop(1, 64, step, 0)
-        own_block = pltpu.make_async_copy(wq.at[tg, zl, h], wr.at[h, zl * N + tg], loc.at[10 + h])
-        own_block.start()
-        return own_block
-
-    own_blocks = [send_weights(0), send_weights(1)]
     spread_core(0)
     spread_core(1)
+
+    copies[4].wait()
+    copies[5].wait()
+    for k in range(4):
+        sorted_rows = jnp.dot(order[...], stg[k].astype(BF), preferred_element_type=F32)
+        mom[:, k] = sorted_rows.astype(BF).reshape(N, PIECE, WIDTH)
+
+    def send_moments(dzh, dx, dc):
+        to = (zh + dzh) % 2 * 8 + (x + dx) % 4 * 2 + (c + dc) % 2
+        send(mom.at[to], momr.at[tg], ms, mr, (dp, to))
+
+    own_moments = pltpu.make_async_copy(mom.at[tg], momr.at[tg], loc.at[7])
+    own_moments.start()
+
 
     wait_bytes(rows(came[2], e, 0), t1r.at[4])
     spread(2, 0)
@@ -337,15 +333,16 @@
 
         lax.fori_loop(0, 4, step, 0)
 
-    def gradients(m):
+    def far_gradient(m):
         gradient(m, yf)
         send(gp.at[m, yf, upper], relay.at[m, 0], rss.at[m, 0], rsr.at[m, 0], at(dy=1))
         send(gp.at[m, yf, lower], relay.at[m, 1], rss.at[m, 1], rsr.at[m, 1], at(dy=-1))
+
+    def near_gradients(m):
         gradient(m, yr)
         send(gp.at[m, yr, lower], got.at[m, 0, lower], rss.at[m, 2], rsr.at[m, 2], at(dy=1))
         gradient(m, yl)
         send(gp.at[m, yl, upper], got.at[m, 1, upper], rss.at[m, 3], rsr.at[m, 3], at(dy=-1))
-        gradient(m, y)
 
     def relays(m):
         wait_bytes(relay.at[m, 0], rsr.at[m, 0])
@@ -381,18 +378,28 @@
     pass_x(2)
     lax.fori_loop(0, 4, near_half, 0)
     pass_y(1)
-    for p in range(3):
-        end_x(p)
-    lax.fori_loop(0, 2, lambda k, _: (send_moments(1, 2, k), 0)[1], 0)
     end_y(0)
     end_y(1)
     forward(zl)
-    for p in range(3):
-        end_tokens(p)
-        forward(came[p])
-    gradients(0)
-    gradients(1)
+    end_x(0)
+    end_x(1)
+    end_tokens(0)
+    forward(came[0])
+    end_x(2)
+    lax.fori_loop(0, 2, lambda k, _: (send_moments(1, 2, k), 0)[1], 0)
+    for k in range(1, 8):
+        send_moments(0, k // 2, k % 2)
+    end_tokens(1)
+    forward(came[1])
+    end_tokens(2)
+    forward(came[2])
+    far_gradient(0)
+    near_gradients(0)
+    far_gradient(1)
     relays(0)
+    near_gradients(1)
+    gradient(0, y)
+    gradient(1, y)
     relays(1)
     finish(0)
     finish(1)
@@ -526,7 +533,7 @@
         in_specs=[scalar, whole, pl.BlockSpec((2, 4, QUART, 256), lambda i: (0,) * 4)],
         out_specs=(flat, flat, pair, pair),
         scratch_shapes=[pltpu.VMEM((2, ROWS, WIDTH), F32)],
-        compiler_params=pltpu.CompilerParams(vmem_limit_bytes=32 * 2**20),
+        compiler_params=pltpu.CompilerParams(vmem_limit_bytes=60 * 2**20),
         cost_estimate=pl.CostEstimate(
             flops=10_000_000, bytes_accessed=13_000_000, transcendentals=500_000
         ),

time: 165 us -> 146 us (0.88); the launches traced: 163 us -> 146 us
  Pallas kernels: 159 us -> 145 us
  local copies, waits for them, and re-layouts: 2.95 us -> 0 us
    pallas_call x1, Pallas kernels: 154 us -> 138 us  [per_device(): pl.pallas_call(exchange, out_shape=(jax.ShapeDtypeStruct((N, 6, PIECE, WI...]
    unnamed x6 -> x0, local copies, waits for them, and re-layouts: 2.95 us -> none
where the time goes in v3:
time: 146 us
  Pallas kernels  145 us (99%)
    pallas_call x1, Pallas kernels, per_device(): pl.pallas_call(exchange, out_shape=(jax.ShapeDtypeStruct((N, 6, PIECE, WI...  138 us
    pallas_call x1, Pallas kernels, per_device(): pl.pallas_call(update, grid=(8,), out_shape=(jax.ShapeDtypeStruct((ROWS,...  6.88 us

profile of v3, /device:TPU:34, one launch (start us, length us, event | category | flops | bytes accessed | tf_op | source)
XLA Modules:
  0.0 145.5 jit_solution(16118824631183118100)
XLA Ops:
  0.6 138.0 %exchange.1 = (bf16[16,6,16,896]{3,2,1,0:T(8,128)(2,1)}, bf16[2,4,224,256]{3,2,1,0:T(8,128)(2,1)}) custom-call(s32[16,16]{1,0:T(8,128)} %bd.1, s32[16]{0:T(128)} %rank.3, bf16[256,4096]{1,0:T(8,128)(2,1)} %tok.1, bf16[256,4096]{1,0:T(8,128)(2,1)} %cot.1, bf16[256,896]{1,0:T(8,128)(2,1)} %upk.1, bf16[256,896]{1,0:T(8,128)(2,1)} %dnk.1, f32[2,256,896]{2,1,0:T(8,128)} %fst.1, ...), custom_call_target="tpu_custom_call" | custom-call | flops 7600000000 | bytes 20000000 | tf_op jit(solution)/shard_map/exchange/pallas_call | solution.py:468
  138.6 6.9 %update.1 = (bf16[256,896]{1,0:T(8,128)(2,1)}, bf16[256,896]{1,0:T(8,128)(2,1)}, f32[2,256,896]{2,1,0:T(8,128)}, f32[2,256,896]{2,1,0:T(8,128)}) custom-call(s32[16]{0:T(128)} %rank.3, bf16[16,6,16,896]{3,2,1,0:T(8,128)(2,1)} %get-tuple-element.6.momr, bf16[2,4,224,256]{3,2,1,0:T(8,128)(2,1)} %get-tuple-element.7.gin), custom_call_target="tpu_custom_call" | custom-call | flops 10000000 | bytes 13000000 | tf_op jit(solution)/shard_map/update/pallas_call | solution.py:524

commit v4 on v3

--- a/solution.py
+++ b/solution.py
@@ -442,8 +442,8 @@
                 ], axis=0)
                 grad[m, lanes, :] = tall.T
 
-    for half in range(2):
-        r = step * 2 + half
+    for half in range(4):
+        r = step * 4 + half
         src = jnp.int32(0)
         for k in range(N):
             src = src + jnp.where((rank[k] + tg) % N == r, k, 0)
@@ -519,11 +519,11 @@
     )(bd, rank, tok, cot, upk, dnk, fst, snd)
 
     whole = pl.BlockSpec((N, 6, PIECE, WIDTH), lambda i: (0, 0, 0, 0))
-    flat = pl.BlockSpec((32, WIDTH), lambda i: (i, 0))
-    pair = pl.BlockSpec((2, 32, WIDTH), lambda i: (0, i, 0))
+    flat = pl.BlockSpec((64, WIDTH), lambda i: (i, 0))
+    pair = pl.BlockSpec((2, 64, WIDTH), lambda i: (0, i, 0))
     return pl.pallas_call(
         update,
-        grid=(8,),
+        grid=(4,),
         out_shape=(
             jax.ShapeDtypeStruct((ROWS, WIDTH), BF),
             jax.ShapeDtypeStruct((ROWS, WIDTH), BF),

time: 146 us -> 144 us (0.986)
  no operation moved by 1% of the time
where the time goes in v4:
time: 144 us
  Pallas kernels  144 us (100%)
    pallas_call x1, Pallas kernels, per_device(): pl.pallas_call(exchange, out_shape=(jax.ShapeDtypeStruct((N, 6, PIECE, WI...  138 us
    pallas_call x1, Pallas kernels, per_device(): pl.pallas_call(update, grid=(4,), out_shape=(jax.ShapeDtypeStruct((ROWS,...  5.67 us

profile of v4, /device:TPU:34, one launch (start us, length us, event | category | flops | bytes accessed | tf_op | source)
XLA Modules:
  0.0 144.3 jit_solution(6059956689363518702)
XLA Ops:
  0.6 138.0 %exchange.1 = (bf16[16,6,16,896]{3,2,1,0:T(8,128)(2,1)}, bf16[2,4,224,256]{3,2,1,0:T(8,128)(2,1)}) custom-call(s32[16,16]{1,0:T(8,128)} %bd.1, s32[16]{0:T(128)} %rank.3, bf16[256,4096]{1,0:T(8,128)(2,1)} %tok.1, bf16[256,4096]{1,0:T(8,128)(2,1)} %cot.1, bf16[256,896]{1,0:T(8,128)(2,1)} %upk.1, bf16[256,896]{1,0:T(8,128)(2,1)} %dnk.1, f32[2,256,896]{2,1,0:T(8,128)} %fst.1, ...), custom_call_target="tpu_custom_call" | custom-call | flops 7600000000 | bytes 20000000 | tf_op jit(solution)/shard_map/exchange/pallas_call | solution.py:468
  138.6 5.7 %update.1 = (bf16[256,896]{1,0:T(8,128)(2,1)}, bf16[256,896]{1,0:T(8,128)(2,1)}, f32[2,256,896]{2,1,0:T(8,128)}, f32[2,256,896]{2,1,0:T(8,128)}) custom-call(s32[16]{0:T(128)} %rank.3, bf16[16,6,16,896]{3,2,1,0:T(8,128)(2,1)} %get-tuple-element.6.momr, bf16[2,4,224,256]{3,2,1,0:T(8,128)(2,1)} %get-tuple-element.7.gin), custom_call_target="tpu_custom_call" | custom-call | flops 10000000 | bytes 13000000 | tf_op jit(solution)/shard_map/update/pallas_call | solution.py:524

commit v5 on v4

--- a/solution.py
+++ b/solution.py
@@ -442,8 +442,8 @@
                 ], axis=0)
                 grad[m, lanes, :] = tall.T
 
-    for half in range(4):
-        r = step * 4 + half
+    for half in range(8):
+        r = step * 8 + half
         src = jnp.int32(0)
         for k in range(N):
             src = src + jnp.where((rank[k] + tg) % N == r, k, 0)
@@ -519,11 +519,11 @@
     )(bd, rank, tok, cot, upk, dnk, fst, snd)
 
     whole = pl.BlockSpec((N, 6, PIECE, WIDTH), lambda i: (0, 0, 0, 0))
-    flat = pl.BlockSpec((64, WIDTH), lambda i: (i, 0))
-    pair = pl.BlockSpec((2, 64, WIDTH), lambda i: (0, i, 0))
+    flat = pl.BlockSpec((128, WIDTH), lambda i: (i, 0))
+    pair = pl.BlockSpec((2, 128, WIDTH), lambda i: (0, i, 0))
     return pl.pallas_call(
         update,
-        grid=(4,),
+        grid=(2,),
         out_shape=(
             jax.ShapeDtypeStruct((ROWS, WIDTH), BF),
             jax.ShapeDtypeStruct((ROWS, WIDTH), BF),

time: 144 us -> 144 us (level)
  no operation moved by 1% of the time
where the time goes in v5:
time: 144 us
  Pallas kernels  143 us (99%)
    pallas_call x1, Pallas kernels, per_device(): pl.pallas_call(exchange, out_shape=(jax.ShapeDtypeStruct((N, 6, PIECE, WI...  138 us
    pallas_call x1, Pallas kernels, per_device(): pl.pallas_call(update, grid=(2,), out_shape=(jax.ShapeDtypeStruct((ROWS,...  5.36 us

profile of v5, /device:TPU:34, one launch (start us, length us, event | category | flops | bytes accessed | tf_op | source)
XLA Modules:
  0.0 144.0 jit_solution(12133508801888854898)
XLA Ops:
  0.6 138.0 %exchange.1 = (bf16[16,6,16,896]{3,2,1,0:T(8,128)(2,1)}, bf16[2,4,224,256]{3,2,1,0:T(8,128)(2,1)}) custom-call(s32[16,16]{1,0:T(8,128)} %bd.1, s32[16]{0:T(128)} %rank.3, bf16[256,4096]{1,0:T(8,128)(2,1)} %tok.1, bf16[256,4096]{1,0:T(8,128)(2,1)} %cot.1, bf16[256,896]{1,0:T(8,128)(2,1)} %upk.1, bf16[256,896]{1,0:T(8,128)(2,1)} %dnk.1, f32[2,256,896]{2,1,0:T(8,128)} %fst.1, ...), custom_call_target="tpu_custom_call" | custom-call | flops 7600000000 | bytes 20000000 | tf_op jit(solution)/shard_map/exchange/pallas_call | solution.py:468
  138.6 5.4 %update.1 = (bf16[256,896]{1,0:T(8,128)(2,1)}, bf16[256,896]{1,0:T(8,128)(2,1)}, f32[2,256,896]{2,1,0:T(8,128)}, f32[2,256,896]{2,1,0:T(8,128)}) custom-call(s32[16]{0:T(128)} %rank.3, bf16[16,6,16,896]{3,2,1,0:T(8,128)(2,1)} %get-tuple-element.6.momr, bf16[2,4,224,256]{3,2,1,0:T(8,128)(2,1)} %get-tuple-element.7.gin), custom_call_target="tpu_custom_call" | custom-call | flops 10000000 | bytes 13000000 | tf_op jit(solution)/shard_map/update/pallas_call | solution.py:524
